TPU v7x, 32 devices: a whole 2x2x4 slice. The times are simulated.
32 devices in a mesh: rep: 2 (over core), tx: 4 (over y, x), ty: 4 (over z).
Axes of the slice: x: 2, y: 2, z: 4, core: 2. Of those that a mesh axis runs over, the one named last changes fastest.
Arguments:
- queries: bfloat16 [2, 32, 32, 4, 384], P('rep', 'tx', 'ty'), may hold values from -8 to 8
- keys: bfloat16 [2, 32, 32, 4, 384], P('rep', 'tx', 'ty'), may hold values from -8 to 8
- values: bfloat16 [2, 32, 32, 4, 384], P('rep', 'tx', 'ty'), may hold values from -6 to 6
- grad_out: bfloat16 [2, 32, 32, 4, 768], P('rep', 'tx', 'ty'), may hold values from -6 to 6
- w_out: bfloat16 [384, 768], replicated, may hold values from -0.3125 to 0.3125
- fluid_count: int32 [4, 4], P('tx', 'ty'), may hold values from 64 to 256, as said below
Outputs:
- grad_q: bfloat16 [2, 32, 32, 4, 384], P('rep', 'tx', 'ty')
- grad_k: bfloat16 [2, 32, 32, 4, 384], P('rep', 'tx', 'ty')
- grad_v: bfloat16 [2, 32, 32, 4, 384], P('rep', 'tx', 'ty')
- grad_w: float32 [384, 768], replicated
Inputs may be any that keep to these rules, and one draw needn't show every extreme that they name: `fluid_count`: some window has 256 fluid cells and another 8 * 8 in every draw.
All inputs are finite; a program needn't handle non-finite values.
Results may differ from a plain program's by a relative error of at most 0.011.
Values may be sent and summed in bfloat16 or wider, within the bound.
A program may use at most 64 MiB of HBM per device.

v0:
```python
import math

import jax
import jax.numpy as jnp
from jax import lax
from jax.sharding import PartitionSpec as P

HEAD_DIM = 32


NEG_FILL = -1e30


def from_behind(block, axis, distance):
    devices = range(lax.axis_size(axis))
    route = [((i - distance) % len(devices), i) for i in devices]
    return lax.ppermute(block, axis, route)


def window_grads(q_rows, k_rows, v_rows, d_rows, fluid_total):
    row_count = q_rows.shape[0]
    head_count = q_rows.shape[1] // HEAD_DIM
    group_size = min(4, head_count)
    score_scale = HEAD_DIM ** (-0.5)
    is_fluid = lax.iota(jnp.int32, row_count) < fluid_total
    attn_parts = []
    query_parts = []
    key_parts = []
    value_parts = []
    for head_start in range(0, head_count, group_size):
        col_start = head_start * HEAD_DIM
        col_end = (head_start + group_size) * HEAD_DIM
        query_heads = q_rows[:, col_start:col_end].reshape(row_count, group_size, HEAD_DIM)
        key_heads = k_rows[:, col_start:col_end].reshape(row_count, group_size, HEAD_DIM)
        value_heads = v_rows[:, col_start:col_end].reshape(row_count, group_size, HEAD_DIM)
        grad_heads = d_rows[:, col_start:col_end].reshape(row_count, group_size, HEAD_DIM)
        scores = (
            jnp.einsum("qhd,khd->hqk", query_heads, key_heads, preferred_element_type=jnp.float32)
            * score_scale
        )
        scores = jnp.where(is_fluid[None, None, :], scores, NEG_FILL)
        row_peak = jnp.max(scores, axis=2, keepdims=True)
        exponent = jnp.exp(scores - row_peak)
        soft_weights = exponent / jnp.sum(exponent, axis=2, keepdims=True)
        soft_weights = jnp.where(is_fluid[None, :, None], soft_weights, 0.0)
        weights_low = soft_weights.astype(jnp.bfloat16)
        attn_out = jnp.einsum(
            "hqk,khd->qhd", weights_low, value_heads, preferred_element_type=jnp.float32
        )
        grad_weights = jnp.einsum(
            "qhd,khd->hqk", grad_heads, value_heads, preferred_element_type=jnp.float32
        )
        row_delta = jnp.sum(soft_weights * grad_weights, axis=2, keepdims=True)
        grad_scores = (soft_weights * (grad_weights - row_delta)).astype(jnp.bfloat16)
        grad_value = jnp.einsum(
            "hqk,qhd->khd", weights_low, grad_heads, preferred_element_type=jnp.float32
        )
        grad_query = (
            jnp.einsum("hqk,khd->qhd", grad_scores, key_heads, preferred_element_type=jnp.float32)
            * score_scale
        )
        grad_key = (
            jnp.einsum("hqk,qhd->khd", grad_scores, query_heads, preferred_element_type=jnp.float32)
            * score_scale
        )
        width = group_size * HEAD_DIM
        attn_parts.append(attn_out.reshape(row_count, width))
        query_parts.append(grad_query.reshape(row_count, width))
        key_parts.append(grad_key.reshape(row_count, width))
        value_parts.append(grad_value.reshape(row_count, width))
    return (
        jnp.concatenate(attn_parts, axis=1),
        jnp.concatenate(query_parts, axis=1),
        jnp.concatenate(key_parts, axis=1),
        jnp.concatenate(value_parts, axis=1),
    )


def local(queries, keys, values, grad_out, w_out, fluid_count):
    side_cells = queries.shape[1]
    depth_cells = queries.shape[3]
    half = side_cells // 2
    fields = (queries, keys, values, grad_out)
    arrived = from_behind(
        (queries[:, :half], keys[:, :half], values[:, :half], grad_out[:, :half]), "tx", -1
    )
    extended = tuple(
        (jnp.concatenate([own[:, half:], got], axis=1) for own, got in zip(fields, arrived))
    )
    moved = from_behind(
        (
            extended[0][:, :, :half],
            extended[1][:, :, :half],
            extended[2][:, :, :half],
            extended[3][:, :, :half],
        ),
        "ty",
        -1,
    )
    shifted = tuple(
        (jnp.concatenate([ext[:, :, half:], got], axis=2) for ext, got in zip(extended, moved))
    )
    grid_shape = shifted[0].shape
    row_count = side_cells * side_cells * depth_cells
    q_rows = shifted[0].reshape(row_count, -1)
    k_rows = shifted[1].reshape(row_count, -1)
    v_rows = shifted[2].reshape(row_count, -1)
    g_rows = shifted[3].reshape(row_count, -1)
    d_rows = lax.dot_general(
        g_rows, w_out, (((1,), (1,)), ((), ())), preferred_element_type=jnp.float32
    ).astype(jnp.bfloat16)
    fluid_total = fluid_count[0, 0]
    attn_out, grad_query, grad_key, grad_value = window_grads(
        q_rows, k_rows, v_rows, d_rows, fluid_total
    )
    attn_low = attn_out.astype(jnp.bfloat16)
    term = lax.dot_general(
        attn_low, g_rows, (((0,), (0,)), ((), ())), preferred_element_type=jnp.float32
    )
    back_shape = grid_shape[:-1] + (grad_query.shape[1],)
    window_out = (
        grad_query.astype(jnp.bfloat16).reshape(back_shape),
        grad_key.astype(jnp.bfloat16).reshape(back_shape),
        grad_value.astype(jnp.bfloat16).reshape(back_shape),
    )
    moved_back = from_behind(
        (window_out[0][:, :, half:], window_out[1][:, :, half:], window_out[2][:, :, half:]),
        "ty",
        1,
    )
    y_layer = tuple(
        (
            jnp.concatenate([got, mine[:, :, :half]], axis=2)
            for got, mine in zip(moved_back, window_out)
        )
    )
    moved_home = from_behind(
        (y_layer[0][:, half:], y_layer[1][:, half:], y_layer[2][:, half:]), "tx", 1
    )
    final = tuple(
        (jnp.concatenate([got, mine[:, :half]], axis=1) for got, mine in zip(moved_home, y_layer))
    )
    cell_total = (
        row_count
        * queries.shape[0]
        * lax.axis_size("rep")
        * lax.axis_size("tx")
        * lax.axis_size("ty")
    )
    grad_w = lax.psum(term, ("rep", "tx", "ty")) * (1.0 / math.sqrt(cell_total))
    return (final[0], final[1], final[2], grad_w)


def solution(mesh):
    placed = (
        P("rep", "tx", "ty", None, None),
        P("rep", "tx", "ty", None, None),
        P("rep", "tx", "ty", None, None),
        P("rep", "tx", "ty", None, None),
        P(),
        P("tx", "ty"),
    )
    return jax.shard_map(
        local,
        mesh=mesh,
        in_specs=placed,
        out_specs=(
            P("rep", "tx", "ty", None, None),
            P("rep", "tx", "ty", None, None),
            P("rep", "tx", "ty", None, None),
            P(),
        ),
        check_vma=False,
    )
```

profile of v0, /device:TPU:1, one launch (start us, length us, event | category | flops | bytes accessed | tf_op | source)
XLA Modules:
  0.0 200.9 jit_solution(2868462882574896138)
XLA Ops:
  7.2 1.1 fusion.69
  8.3 3.0 %collective-permute-start = (bf16[1,4,8,4,384]{4,3,2,1,0:T(4,128)(2,1)S(1)}, bf16[1,4,8,4,384]{4,3,2,1,0:T(4,128)(2,1)S(1)}, u32[]{:S(2)}, u32[]{:S(2)}) collective-permute-start(bf16[1,4,8,4,384]{4,3,2,1,0:T(4,128)(2,1)S(1)} %get-tuple-element.40), channel_id=1, source_target_pairs={{4,0},{8,4},{12,8},{0,12},{5,1},{9,5},{13,9},{1,13},{6,2},{10,6},{... | collective-permute-start | bytes 294920 | tf_op jit(solution)/shard_map/ppermute | solution.py:17
  11.4 1.0 fusion.67
  12.4 0.3 collective-permute-start.2
  12.7 1.2 fusion.59
  13.9 1.2 collective-permute-start.4
  16.1 3.6 %collective-permute-start.1 = (bf16[1,8,4,4,384]{4,3,2,1,0:T(4,128)(2,1)S(1)}, bf16[1,8,4,4,384]{4,3,2,1,0:T(4,128)(2,1)S(1)}, u32[]{:S(2)}, u32[]{:S(2)}) collective-permute-start(bf16[1,8,4,4,384]{4,3,2,1,0:T(4,128)(2,1)S(1)} %get-tuple-element.38), channel_id=1, source_target_pairs={{1,0},{2,1},{3,2},{0,3},{5,4},{6,5},{7,6},{4,7},{9,8},{10,9},{11,1... | collective-permute-start | bytes 294920 | tf_op jit(solution)/shard_map/ppermute | solution.py:17
  19.8 0.2 collective-permute-start.3
  20.0 2.9 %collective-permute-done.6 = bf16[1,4,8,4,384]{4,3,2,1,0:T(4,128)(2,1)S(1)} collective-permute-done((bf16[1,4,8,4,384]{4,3,2,1,0:T(4,128)(2,1)S(1)}, bf16[1,4,8,4,384]{4,3,2,1,0:T(4,128)(2,1)S(1)}, u32[]{:S(2)}, u32[]{:S(2)}) %collective-permute-start.6) | collective-permute-done | bytes 98336 | tf_op jit(solution)/shard_map/ppermute | solution.py:17
  23.1 3.4 %collective-permute-start.7 = (bf16[1,8,4,4,384]{4,3,2,1,0:T(4,128)(2,1)S(1)}, bf16[1,8,4,4,384]{4,3,2,1,0:T(4,128)(2,1)S(1)}, u32[]{:S(2)}, u32[]{:S(2)}) collective-permute-start(bf16[1,8,4,4,384]{4,3,2,1,0:T(4,128)(2,1)S(1)} %get-tuple-element.34), channel_id=1, source_target_pairs={{1,0},{2,1},{3,2},{0,3},{5,4},{6,5},{7,6},{4,7},{9,8},{10,9},{11,1... | collective-permute-start | bytes 294920 | tf_op jit(solution)/shard_map/ppermute | solution.py:17
  27.3 0.3 fusion.33
  27.6 0.2 collective-permute-start.5
  27.8 0.3 collective-permute-done.7
  29.0 1.5 fusion.70
  30.5 1.5 fusion.71
  32.0 1.5 fusion.72
  33.6 1.3 convolution_convert_fusion.1
  34.9 1.3 convolution_convert_fusion.2
  36.2 1.3 convolution_convert_fusion.3
  37.5 0.3 pad_maximum_fusion
  37.9 0.4 convolution_convert_fusion
  38.3 0.7 fusion.66
  39.1 0.3 fusion.74
  39.4 0.7 copy.48
  40.2 1.2 fusion.73
  41.4 1.6 copy.60
  42.9 2.6 %multiply_reduce_fusion = (f32[4,256]{1,0:T(4,128)S(1)}, f32[4,256]{1,0:T(4,128)S(1)}, f32[4,256]{1,0:T(4,128)S(1)}, f32[4,256,256]{1,2,0:T(8,128)S(1)}) fusion(f32[4,256,256]{1,2,0:T(8,128)} %get-tuple-element.45, f32[4,256]{1,0:T(4,128)S(1)} %get-tuple-element.44, pred[256]{0:T(512)(128)(4,1)S(1)} %iota_compare_fusion, f32[4,256,256]{1,2,0:T(8,128)S(1)} %fusion.74, ...), kind=kOutput, calls=%fused_computation.44 | convolution fusion | flops 19919872 | bytes 6447360 | tf_op jit(solution)/shard_map/qhd,khd->hqk/dot_general | solution.py:50
  45.6 0.2 copy-done.3
  45.8 0.6 multiply_convert_fusion
  46.4 0.2 fusion.23
  46.6 0.3 fusion.20
  46.9 0.2 fusion.22
  47.1 0.3 fusion.19
  47.3 0.2 fusion.21
  47.6 0.3 fusion.18
  47.8 0.7 fusion.24
  48.5 0.7 fusion.25
  49.4 0.7 fusion.26
  50.1 0.2 copy.51
  50.3 0.2 concatenate.105
  50.5 0.2 copy.57
  50.7 0.2 concatenate.106
  50.9 0.2 copy.63
  51.0 0.2 concatenate.107
  51.4 1.2 collective-permute-start.8
  52.6 0.2 copy.65
  53.0 0.2 copy.67
  53.4 0.2 copy.69
  54.1 0.2 copy.71
  54.5 0.2 copy.73
  54.9 0.2 copy.75
  55.1 0.2 concatenate.119
  55.4 3.1 %collective-permute-start.12 = (bf16[1,8,4,4,384]{4,3,2,1,0:T(4,128)(2,1)S(1)}, bf16[1,8,4,4,384]{4,3,2,1,0:T(4,128)(2,1)S(1)}, u32[]{:S(2)}, u32[]{:S(2)}) collective-permute-start(bf16[1,8,4,4,384]{4,3,2,1,0:T(4,128)(2,1)S(1)} %get-tuple-element.11), channel_id=1, source_target_pairs={{3,0},{0,1},{1,2},{2,3},{7,4},{4,5},{5,6},{6,7},{11,8},{8,9},{9,10... | collective-permute-start | bytes 294920 | tf_op jit(solution)/shard_map/ppermute | solution.py:17
  58.6 1.3 fusion.37
  60.0 0.4 collective-permute-start.9
  60.5 1.1 collective-permute-start.11
  61.6 0.2 collective-permute-done.12
  61.9 1.4 collective-permute-start.13
  63.3 1.4 collective-permute-done.9
  64.7 0.8 fusion.36
  65.6 0.8 fusion.35
  66.5 0.8 fusion.34
  67.4 124.3 %all-reduce.2.cloned.1.call-done = f32[384,768]{1,0:T(8,128)} async-done(((f32[384,768]{1,0:T(8,128)}), f32[384,768]{1,0:T(8,128)}) %all-reduce.2.cloned.1.call-update) | async-done | bytes 1179664 | tf_op jit(solution)/shard_map/psum | solution.py:150
  191.7 2.4 %broadcast_multiply_fusion = f32[384,768]{1,0:T(8,128)} fusion(f32[384,768]{1,0:T(8,128)} %all-reduce.2.cloned.1.call-done), kind=kLoop, calls=%fused_computation.52 | loop fusion | flops 294912 | bytes 2359296 | tf_op jit(solution)/shard_map/mul | solution.py:150
  (82 shorter events, 4.6 us)
Async XLA Ops:
  7.2 30.7 %copy-start = (bf16[384,768]{1,0:T(8,128)(2,1)S(1)}, bf16[384,768]{1,0:T(8,128)(2,1)}, u32[]{:S(2)}) copy-start(bf16[384,768]{1,0:T(8,128)(2,1)} %param.10) | copy-start | bytes 1769476
  7.2 7.9 %copy-start.6 = (bf16[1,8,8,4,384]{4,3,2,1,0:T(4,128)(2,1)S(1)}, bf16[1,8,8,4,384]{4,3,2,1,0:T(4,128)(2,1)}, u32[]{:S(2)}) copy-start(bf16[1,8,8,4,384]{4,3,2,1,0:T(4,128)(2,1)} %param.8) | copy-start | bytes 589828
  7.2 184.5 %all-reduce.2.cloned.1.call-start = ((), (), s32[]{:S(2)}) async-start(), calls=%async_computation | async-start | bytes 2359296 | tf_op jit(solution)/shard_map/psum | solution.py:150
  8.3 7.6 %collective-permute-start = (bf16[1,4,8,4,384]{4,3,2,1,0:T(4,128)(2,1)S(1)}, bf16[1,4,8,4,384]{4,3,2,1,0:T(4,128)(2,1)S(1)}, u32[]{:S(2)}, u32[]{:S(2)}) collective-permute-start(bf16[1,4,8,4,384]{4,3,2,1,0:T(4,128)(2,1)S(1)} %get-tuple-element.40), channel_id=1, source_target_pairs={{4,0},{8,4},{12,8},{0,12},{5,1},{9,5},{13,9},{1,13},{6,2},{10,6},{... | collective-permute-start | bytes 294920 | tf_op jit(solution)/shard_map/ppermute | solution.py:17
  12.4 7.3 %collective-permute-start.2 = (bf16[1,4,8,4,384]{4,3,2,1,0:T(4,128)(2,1)S(1)}, bf16[1,4,8,4,384]{4,3,2,1,0:T(4,128)(2,1)S(1)}, u32[]{:S(2)}, u32[]{:S(2)}) collective-permute-start(bf16[1,4,8,4,384]{4,3,2,1,0:T(4,128)(2,1)S(1)} %get-tuple-element.32), channel_id=1, source_target_pairs={{4,0},{8,4},{12,8},{0,12},{5,1},{9,5},{13,9},{1,13},{6,2},{10,6},{... | collective-permute-start | bytes 294920 | tf_op jit(solution)/shard_map/ppermute | solution.py:17
  13.9 13.4 %collective-permute-start.4 = (bf16[1,4,8,4,768]{4,3,2,1,0:T(4,128)(2,1)S(1)}, bf16[1,4,8,4,768]{4,3,2,1,0:T(4,128)(2,1)S(1)}, u32[]{:S(2)}, u32[]{:S(2)}) collective-permute-start(bf16[1,4,8,4,768]{4,3,2,1,0:T(4,128)(2,1)S(1)} %get-tuple-element.10), channel_id=1, source_target_pairs={{4,0},{8,4},{12,8},{0,12},{5,1},{9,5},{13,9},{1,13},{6,2},{10,6},{... | collective-permute-start | bytes 589832 | tf_op jit(solution)/shard_map/ppermute | solution.py:17
  15.2 7.8 %collective-permute-start.6 = (bf16[1,4,8,4,384]{4,3,2,1,0:T(4,128)(2,1)S(1)}, bf16[1,4,8,4,384]{4,3,2,1,0:T(4,128)(2,1)S(1)}, u32[]{:S(2)}, u32[]{:S(2)}) collective-permute-start(bf16[1,4,8,4,384]{4,3,2,1,0:T(4,128)(2,1)S(1)} %get-tuple-element.36), channel_id=1, source_target_pairs={{4,0},{8,4},{12,8},{0,12},{5,1},{9,5},{13,9},{1,13},{6,2},{10,6},{... | collective-permute-start | bytes 294920 | tf_op jit(solution)/shard_map/ppermute | solution.py:17
  16.1 10.4 %collective-permute-start.1 = (bf16[1,8,4,4,384]{4,3,2,1,0:T(4,128)(2,1)S(1)}, bf16[1,8,4,4,384]{4,3,2,1,0:T(4,128)(2,1)S(1)}, u32[]{:S(2)}, u32[]{:S(2)}) collective-permute-start(bf16[1,8,4,4,384]{4,3,2,1,0:T(4,128)(2,1)S(1)} %get-tuple-element.38), channel_id=1, source_target_pairs={{1,0},{2,1},{3,2},{0,3},{5,4},{6,5},{7,6},{4,7},{9,8},{10,9},{11,1... | collective-permute-start | bytes 294920 | tf_op jit(solution)/shard_map/ppermute | solution.py:17
  19.8 7.0 %collective-permute-start.3 = (bf16[1,8,4,4,384]{4,3,2,1,0:T(4,128)(2,1)S(1)}, bf16[1,8,4,4,384]{4,3,2,1,0:T(4,128)(2,1)S(1)}, u32[]{:S(2)}, u32[]{:S(2)}) collective-permute-start(bf16[1,8,4,4,384]{4,3,2,1,0:T(4,128)(2,1)S(1)} %get-tuple-element.30), channel_id=1, source_target_pairs={{1,0},{2,1},{3,2},{0,3},{5,4},{6,5},{7,6},{4,7},{9,8},{10,9},{11,1... | collective-permute-start | bytes 294920 | tf_op jit(solution)/shard_map/ppermute | solution.py:17
  23.1 5.0 %collective-permute-start.7 = (bf16[1,8,4,4,384]{4,3,2,1,0:T(4,128)(2,1)S(1)}, bf16[1,8,4,4,384]{4,3,2,1,0:T(4,128)(2,1)S(1)}, u32[]{:S(2)}, u32[]{:S(2)}) collective-permute-start(bf16[1,8,4,4,384]{4,3,2,1,0:T(4,128)(2,1)S(1)} %get-tuple-element.34), channel_id=1, source_target_pairs={{1,0},{2,1},{3,2},{0,3},{5,4},{6,5},{7,6},{4,7},{9,8},{10,9},{11,1... | collective-permute-start | bytes 294920 | tf_op jit(solution)/shard_map/ppermute | solution.py:17
  27.6 10.0 %collective-permute-start.5 = (bf16[1,8,4,4,768]{4,3,2,1,0:T(4,128)(2,1)S(1)}, bf16[1,8,4,4,768]{4,3,2,1,0:T(4,128)(2,1)S(1)}, u32[]{:S(2)}, u32[]{:S(2)}) collective-permute-start(bf16[1,8,4,4,768]{4,3,2,1,0:T(4,128)(2,1)S(1)} %get-tuple-element.8), channel_id=1, source_target_pairs={{1,0},{2,1},{3,2},{0,3},{5,4},{6,5},{7,6},{4,7},{9,8},{10,9},{11,1... | collective-permute-start | bytes 589832 | tf_op jit(solution)/shard_map/ppermute | solution.py:17
  28.8 7.4 %copy-start.5 = (bf16[256,128]{0,1:T(8,128)(2,1)}, bf16[256,128]{0,1:T(8,128)(2,1)S(1)}, u32[]{:S(2)}) copy-start(bf16[256,128]{0,1:T(8,128)(2,1)S(1)} %copy.93) | copy-start | bytes 196612
  29.0 4.6 %copy-start.11 = (bf16[256,128]{0,1:T(8,128)(2,1)}, bf16[256,128]{0,1:T(8,128)(2,1)S(1)}, u32[]{:S(2)}) copy-start(bf16[256,128]{0,1:T(8,128)(2,1)S(1)} %copy.99) | copy-start | bytes 196612
  42.9 2.7 %copy-start.1 = (f32[4,256,256]{1,2,0:T(8,128)S(1)}, f32[4,256,256]{1,2,0:T(8,128)}, u32[]{:S(2)}) copy-start(f32[4,256,256]{1,2,0:T(8,128)} %get-tuple-element.45) | copy-start | bytes 3145732
  42.9 2.7 %copy-start.2 = (f32[4,256,256]{1,2,0:T(8,128)S(1)}, f32[4,256,256]{1,2,0:T(8,128)}, u32[]{:S(2)}) copy-start(f32[4,256,256]{1,2,0:T(8,128)} %get-tuple-element.47) | copy-start | bytes 3145732
  42.9 2.8 %copy-start.3 = (f32[4,256,256]{1,2,0:T(8,128)S(1)}, f32[4,256,256]{1,2,0:T(8,128)}, u32[]{:S(2)}) copy-start(f32[4,256,256]{1,2,0:T(8,128)} %get-tuple-element.49) | copy-start | bytes 3145732
  46.9 1.0 copy-start.4
  48.5 0.9 copy-start.10
  51.4 8.5 %collective-permute-start.8 = (bf16[1,8,4,4,384]{4,3,2,1,0:T(4,128)(2,1)S(1)}, bf16[1,8,4,4,384]{4,3,2,1,0:T(4,128)(2,1)S(1)}, u32[]{:S(2)}, u32[]{:S(2)}) collective-permute-start(bf16[1,8,4,4,384]{4,3,2,1,0:T(4,128)(2,1)S(1)} %get-tuple-element.15), channel_id=1, source_target_pairs={{3,0},{0,1},{1,2},{2,3},{7,4},{4,5},{5,6},{6,7},{11,8},{8,9},{9,10... | collective-permute-start | bytes 294920 | tf_op jit(solution)/shard_map/ppermute | solution.py:17
  53.9 6.5 %collective-permute-start.10 = (bf16[1,8,4,4,384]{4,3,2,1,0:T(4,128)(2,1)S(1)}, bf16[1,8,4,4,384]{4,3,2,1,0:T(4,128)(2,1)S(1)}, u32[]{:S(2)}, u32[]{:S(2)}) collective-permute-start(bf16[1,8,4,4,384]{4,3,2,1,0:T(4,128)(2,1)S(1)} %get-tuple-element.13), channel_id=1, source_target_pairs={{3,0},{0,1},{1,2},{2,3},{7,4},{4,5},{5,6},{6,7},{11,8},{8,9},{9,10... | collective-permute-start | bytes 294920 | tf_op jit(solution)/shard_map/ppermute | solution.py:17
  54.3 4.3 %copy-start.7 = (bf16[4,32,256]{2,1,0:T(8,128)(2,1)S(1)}, bf16[4,32,256]{2,1,0:T(8,128)(2,1)}, u32[]{:S(2)}) copy-start(bf16[4,32,256]{2,1,0:T(8,128)(2,1)} %convolution_convert_fusion.1) | copy-start | bytes 196612
  54.3 4.3 %copy-start.8 = (bf16[4,32,256]{2,1,0:T(8,128)(2,1)S(1)}, bf16[4,32,256]{2,1,0:T(8,128)(2,1)}, u32[]{:S(2)}) copy-start(bf16[4,32,256]{2,1,0:T(8,128)(2,1)} %convolution_convert_fusion.2) | copy-start | bytes 196612
  54.3 4.3 %copy-start.9 = (bf16[4,32,256]{2,1,0:T(8,128)(2,1)S(1)}, bf16[4,32,256]{2,1,0:T(8,128)(2,1)}, u32[]{:S(2)}) copy-start(bf16[4,32,256]{2,1,0:T(8,128)(2,1)} %convolution_convert_fusion.3) | copy-start | bytes 196612
  55.4 6.4 %collective-permute-start.12 = (bf16[1,8,4,4,384]{4,3,2,1,0:T(4,128)(2,1)S(1)}, bf16[1,8,4,4,384]{4,3,2,1,0:T(4,128)(2,1)S(1)}, u32[]{:S(2)}, u32[]{:S(2)}) collective-permute-start(bf16[1,8,4,4,384]{4,3,2,1,0:T(4,128)(2,1)S(1)} %get-tuple-element.11), channel_id=1, source_target_pairs={{3,0},{0,1},{1,2},{2,3},{7,4},{4,5},{5,6},{6,7},{11,8},{8,9},{9,10... | collective-permute-start | bytes 294920 | tf_op jit(solution)/shard_map/ppermute | solution.py:17
  60.0 4.7 %collective-permute-start.9 = (bf16[1,4,8,4,384]{4,3,2,1,0:T(4,128)(2,1)S(1)}, bf16[1,4,8,4,384]{4,3,2,1,0:T(4,128)(2,1)S(1)}, u32[]{:S(2)}, u32[]{:S(2)}) collective-permute-start(bf16[1,4,8,4,384]{4,3,2,1,0:T(4,128)(2,1)S(1)} %fusion.45), channel_id=1, source_target_pairs={{12,0},{0,4},{4,8},{8,12},{13,1},{1,5},{5,9},{9,13},{14,2},{2,6},{... | collective-permute-start | bytes 294920 | tf_op jit(solution)/shard_map/ppermute | solution.py:17
  60.5 5.1 %collective-permute-start.11 = (bf16[1,4,8,4,384]{4,3,2,1,0:T(4,128)(2,1)S(1)}, bf16[1,4,8,4,384]{4,3,2,1,0:T(4,128)(2,1)S(1)}, u32[]{:S(2)}, u32[]{:S(2)}) collective-permute-start(bf16[1,4,8,4,384]{4,3,2,1,0:T(4,128)(2,1)S(1)} %fusion.44), channel_id=1, source_target_pairs={{12,0},{0,4},{4,8},{8,12},{13,1},{1,5},{5,9},{9,13},{14,2},{2,6},{... | collective-permute-start | bytes 294920 | tf_op jit(solution)/shard_map/ppermute | solution.py:17
  61.9 4.6 %collective-permute-start.13 = (bf16[1,4,8,4,384]{4,3,2,1,0:T(4,128)(2,1)S(1)}, bf16[1,4,8,4,384]{4,3,2,1,0:T(4,128)(2,1)S(1)}, u32[]{:S(2)}, u32[]{:S(2)}) collective-permute-start(bf16[1,4,8,4,384]{4,3,2,1,0:T(4,128)(2,1)S(1)} %fusion.43), channel_id=1, source_target_pairs={{12,0},{0,4},{4,8},{8,12},{13,1},{1,5},{5,9},{9,13},{14,2},{2,6},{... | collective-permute-start | bytes 294920 | tf_op jit(solution)/shard_map/ppermute | solution.py:17
Sparse Core Ops, SparseCore 0:
  60.1 131.5 all-reduce.1
where the time goes:
time: 203 us; the launch traced here: 201 us
  waiting for transfers between devices  129 us (64%)
  starting transfers between devices  19.5 us (10%)
  matrix products  17.8 us (9%)
  between operations  15.4 us (8%)
  local copies, waits for them, and re-layouts  11.9 us (6%)
  other arithmetic  6.95 us (3%)
    psum x1, waiting for transfers between devices, local(): grad_w = lax.psum(term, ('rep', 'tx', 'ty')) * (1.0 / math.sqrt(cell_total))  124 us
    ppermute x14, starting transfers between devices, from_behind(): return lax.ppermute(block, axis, route)  19.5 us
    ppermute x14, waiting for transfers between devices, from_behind(): return lax.ppermute(block, axis, route)  5.1 us
    sub x3, matrix products, window_grads(): exponent = jnp.exp(scores - row_peak)  4.54 us
    dot_general x3, matrix products, window_grads(): jnp.einsum('qhd,khd->hqk', grad_heads, value_heads, preferred_element_typ...  4.18 us
  transfers between devices with their start and end apart: 15, of which 6 were waited for; matrix products, arithmetic and copies ran while one was open for 10% of the time, Pallas kernels for 0%

commit v1 on v0

v1 whole, which is shorter than its diff:
```python
import functools
import math

import jax
import jax.numpy as jnp
from jax import lax
from jax.experimental import pallas as pl
from jax.experimental.pallas import tpu as pltpu
from jax.sharding import PartitionSpec as P

HEAD_DIM = 32
LANES = 128
PER_GROUP = LANES // HEAD_DIM
NEG_FILL = -1e30
MESH = pl.DeviceIdType.MESH
F32 = jnp.float32
BF16 = jnp.bfloat16


def dot(a, b, dims):
    return lax.dot_general(a, b, (dims, ((), ())), preferred_element_type=F32)


def kernel(plan, fluid, q_in, k_in, v_in, g_in, w_ref, oq, ok, ov, ow, *scratch):
    nx, ny, share, cells = plan
    (qw, kw, vw, gw, probs, dw, gq, gk, gv, in_send, in_recv, own_sem, out_send, out_recv) = scratch[:14]
    rep, tx, ty = lax.axis_index("rep"), lax.axis_index("tx"), lax.axis_index("ty")

    def at(dx, dy):
        return {"tx": lax.rem(tx + dx, nx), "ty": lax.rem(ty + dy, ny)}

    ahead = [at(1, 0), at(0, 1), at(1, 1)]
    behind = [at(nx - 1, 0), at(0, ny - 1), at(nx - 1, ny - 1)]
    if share:
        greet = [{"rep": 1 - rep}, ahead[2], behind[2]]
        greet += [at(d, 0) for d in range(1, nx)] + [at(0, d) for d in range(1, ny)]
    else:
        greet = ahead + behind
    barrier = pltpu.get_barrier_semaphore()
    for peer in greet:
        pl.semaphore_signal(barrier, inc=1, device_id=peer, device_id_type=MESH)

    side, row, width = qw.shape
    hs, hr = side // 2, row // 2
    lo = (slice(0, hs), slice(0, hr))
    low_x = (slice(0, hs), slice(hr, row))
    low_y = (slice(hs, side), slice(0, hr))
    high = (slice(hs, side), slice(hr, row))
    leaving = [(low_x, low_y), (low_y, low_x), (lo, high)]

    fields = [(q_in, qw), (k_in, kw), (v_in, vw), (g_in, gw)]
    owns = []
    for f, (src, dst) in enumerate(fields):
        owns.append(pltpu.make_async_copy(src.at[high], dst.at[lo], own_sem.at[f]))
        owns[-1].start()
    pl.semaphore_wait(barrier, len(greet))
    arriving = []
    for f, (src, dst) in enumerate(fields):
        copies = []
        for n, (from_, to) in enumerate(leaving):
            copies.append(
                pltpu.make_async_remote_copy(
                    src_ref=src.at[from_], dst_ref=dst.at[to],
                    send_sem=in_send.at[f, n], recv_sem=in_recv.at[f, n],
                    device_id=behind[n], device_id_type=MESH,
                )
            )
            copies[-1].start()
        arriving.append(copies)

    def arrive(f):
        owns[f].wait()
        for copy in arriving[f]:
            copy.wait_recv()

    cells_here = side * row
    groups = width // LANES
    count = fluid[0, 0]
    key_ok = lax.broadcasted_iota(jnp.int32, (cells_here, 1), 0) < count
    query_ok = jnp.where(lax.broadcasted_iota(jnp.int32, (1, cells_here), 1) < count, 1.0, 0.0)
    lane_head = lax.broadcasted_iota(jnp.int32, (1, LANES), 1) // HEAD_DIM
    pick = [jnp.where(lane_head == h, 1.0, 0.0).astype(BF16) for h in range(PER_GROUP)]
    scale = HEAD_DIM ** (-0.5)

    def part(ref, g):
        return ref[:, :, g * LANES : (g + 1) * LANES].reshape(cells_here, LANES)

    def attend(g):
        keys, queries = part(kw, g), part(qw, g)
        for h in range(PER_GROUP):
            s = dot(keys, queries * pick[h], ((1,), (1,)))
            s = jnp.where(key_ok, s, NEG_FILL)
            e = jnp.exp2((s - jnp.max(s, axis=0, keepdims=True)) * (scale * math.log2(math.e)))
            inv = query_ok / jnp.sum(e, axis=0, keepdims=True)
            probs[g * PER_GROUP + h] = e * inv

    def mix(g):
        values_t = part(vw, g).T
        outs = []
        for h in range(PER_GROUP):
            p = probs[g * PER_GROUP + h].astype(BF16)
            outs.append(dot(values_t[h * HEAD_DIM : (h + 1) * HEAD_DIM], p, ((1,), (0,))))
        attn_t = jnp.concatenate(outs, axis=0).astype(BF16)
        return dot(attn_t, gw[...].reshape(cells_here, -1), ((1,), (0,)))

    def back(g):
        keys, queries, values = part(kw, g), part(qw, g), part(vw, g)
        keys_t = keys.T
        d_rows = dw[g]
        dq, dk, dv = [], 0.0, 0.0
        for h in range(PER_GROUP):
            p = probs[g * PER_GROUP + h]
            d_h, q_h = d_rows * pick[h], queries * pick[h]
            dp = dot(values, d_h, ((1,), (1,)))
            delta = jnp.sum(p * dp, axis=0, keepdims=True)
            ds = (p * (dp - delta)).astype(BF16)
            dv = dv + dot(p.astype(BF16), d_h, ((1,), (0,)))
            dk = dk + dot(ds, q_h, ((1,), (0,)))
            dq.append(dot(keys_t[h * HEAD_DIM : (h + 1) * HEAD_DIM], ds, ((1,), (0,))))
        dq = (jnp.concatenate(dq, axis=0) * scale).T
        at_g = slice(g * LANES, (g + 1) * LANES)
        for ref, out, val in ((gq, oq, dq), (gk, ok, dk * scale), (gv, ov, dv)):
            val = val.astype(BF16).reshape(side, row, LANES)
            ref[:, :, at_g] = val
            out[hs:, hr:, at_g] = val[:hs, :hr]

    returning = []

    def give_back():
        for f, (src, dst) in enumerate(((gq, oq), (gk, ok), (gv, ov))):
            for n, (home, here) in enumerate(leaving):
                returning.append(
                    pltpu.make_async_remote_copy(
                        src_ref=src.at[here], dst_ref=dst.at[home],
                        send_sem=out_send.at[f, n], recv_sem=out_recv.at[f, n],
                        device_id=ahead[n], device_id_type=MESH,
                    )
                )
                returning[-1].start()

    arrive(0)
    arrive(1)
    for g in range(groups):
        attend(g)
    arrive(2)
    arrive(3)
    if share:
        (tb, sb, r0, s1, s1b, r1, s2, r2, a2, a1, a0) = scratch[14:25]
        (rep_s, rep_r, tx_s, tx_r, ty_s, ty_r, gy_s, gy_r, gx_s, gx_r, gr_s, gr_r) = scratch[25:]
    rep_copies = []
    half = w_ref.shape[1] // 2
    for g in range(groups):
        term = mix(g)
        at_g = slice(g * LANES, (g + 1) * LANES)
        if not share:
            ow[at_g, :] = term
            continue
        for c in range(2):
            tb[c, at_g] = term[:, c * half : (c + 1) * half]
            sb[c, at_g] = term[:, c * half : (c + 1) * half].astype(BF16)
        rep_copies.append(
            pltpu.make_async_remote_copy(
                src_ref=sb.at[1 - rep, at_g], dst_ref=r0.at[at_g],
                send_sem=rep_s.at[g], recv_sem=rep_r.at[g],
                device_id={"rep": 1 - rep}, device_id_type=MESH,
            )
        )
        rep_copies[-1].start()
    for g in range(groups):
        dw[g] = dot(gw[...].reshape(cells_here, -1), w_ref[g * LANES : (g + 1) * LANES, :], ((1,), (1,))).astype(BF16)

    sent = []

    def spread(src_of, dst_of, peers, send, recv):
        copies = []
        for d, peer in peers:
            copies.append(
                pltpu.make_async_remote_copy(
                    src_ref=src_of(d), dst_ref=dst_of(d),
                    send_sem=send.at[d - 1], recv_sem=recv.at[d - 1],
                    device_id=peer, device_id_type=MESH,
                )
            )
            copies[-1].start()
        sent.extend(copies)
        return copies

    x_peers = [(d, at(d, 0)) for d in range(1, nx)]
    y_peers = [(d, at(0, d)) for d in range(1, ny)]

    back(0)
    if share:
        for copy in rep_copies:
            copy.wait_recv()
        total = tb[rep] + r0[...].astype(F32)
        s1[...] = total.reshape(s1.shape)
        s1b[...] = total.astype(BF16).reshape(s1.shape)
        x_copies = spread(
            lambda d: s1b.at[lax.rem(tx + d, nx)], lambda d: r1.at[d - 1], x_peers, tx_s, tx_r
        )
    back(1)
    if share:
        total = s1[tx]
        for d, copy in enumerate(x_copies):
            copy.wait_recv()
            total = total + r1[d].astype(F32)
        s2[...] = total.reshape(s2.shape)
        y_copies = spread(
            lambda d: s2.at[lax.rem(ty + d, ny)], lambda d: r2.at[d - 1], y_peers, ty_s, ty_r
        )
    back(2)
    for g in range(3, groups):
        back(g)
    give_back()
    if share:
        total = s2[ty]
        for d, copy in enumerate(y_copies):
            copy.wait_recv()
            total = total + r2[d]
        a2[ty] = total * (1.0 / math.sqrt(cells))
        for copy in spread(lambda d: a2.at[ty], lambda d: a2.at[ty], y_peers, gy_s, gy_r):
            copy.wait_recv()
        a1[tx] = a2[...].reshape(a1.shape[1:]).astype(BF16)
        for copy in spread(lambda d: a1.at[tx], lambda d: a1.at[tx], x_peers, gx_s, gx_r):
            copy.wait_recv()
        a0[rep] = a1[...].reshape(a0.shape[1:])
        last = pltpu.make_async_remote_copy(
            src_ref=a0.at[rep], dst_ref=a0.at[rep], send_sem=gr_s, recv_sem=gr_r,
            device_id={"rep": 1 - rep}, device_id_type=MESH,
        )
        last.start()
        last.wait_recv()
        for c in range(2):
            ow[:, c * half : (c + 1) * half] = a0[c].astype(F32)
        sent.append(last)
    for copy in returning:
        copy.wait_recv()
    for copies in arriving:
        sent.extend(copies)
    for copy in sent + returning + rep_copies:
        copy.wait_send()


def local(sizes, queries, keys, values, grad_out, w_out, fluid_count):
    nr, nx, ny = sizes
    side, depth = queries.shape[1], queries.shape[3]
    row, width, model = side * depth, queries.shape[4], grad_out.shape[4]
    cells = side * row * queries.shape[0] * nr * nx * ny
    share = nr == 2 and width % (nx * ny * 8) == 0
    groups = width // LANES
    half = model // 2
    win = pltpu.VMEM((side, row, width), BF16)
    dma = pltpu.SemaphoreType.DMA
    scratch = [
        win, win, win, pltpu.VMEM((side, row, model), BF16),
        pltpu.VMEM((groups * PER_GROUP, side * row, side * row), F32),
        pltpu.VMEM((groups, side * row, LANES), BF16),
        win, win, win,
        dma((4, 3)), dma((4, 3)), dma((4,)), dma((3, 3)), dma((3, 3)),
    ]
    if share:
        wx = width // nx
        wy = wx // ny
        scratch += [
            pltpu.VMEM((2, width, half), F32), pltpu.VMEM((2, width, half), BF16),
            pltpu.VMEM((width, half), BF16),
            pltpu.VMEM((nx, wx, half), F32), pltpu.VMEM((nx, wx, half), BF16),
            pltpu.VMEM((nx - 1, wx, half), BF16),
            pltpu.VMEM((ny, wy, half), F32), pltpu.VMEM((ny - 1, wy, half), F32),
            pltpu.VMEM((ny, wy, half), F32),
            pltpu.VMEM((nx, wx, half), BF16),
            pltpu.VMEM((2, width, half), BF16),
            dma((groups,)), dma((groups,)),
            dma((nx - 1,)), dma((nx - 1,)), dma((ny - 1,)), dma((ny - 1,)),
            dma((ny - 1,)), dma((ny - 1,)), dma((nx - 1,)), dma((nx - 1,)),
            dma, dma,
        ]
    flat = lambda a: a.reshape(side, row, a.shape[-1])
    vmem = pl.BlockSpec(memory_space=pltpu.VMEM)
    hbm = pl.BlockSpec(memory_space=pl.ANY)
    grad = jax.ShapeDtypeStruct((side, row, width), BF16)
    gq, gk, gv, gw = pl.pallas_call(
        functools.partial(kernel, (nx, ny, share, cells)),
        out_shape=(grad, grad, grad, jax.ShapeDtypeStruct((width, model), F32)),
        in_specs=[pl.BlockSpec(memory_space=pltpu.SMEM), hbm, hbm, hbm, hbm, vmem],
        out_specs=(vmem, vmem, vmem, vmem),
        scratch_shapes=scratch,
        compiler_params=pltpu.CompilerParams(
            collective_id=0, has_side_effects=True, vmem_limit_bytes=40 * 2**20
        ),
    )(fluid_count, flat(queries), flat(keys), flat(values), flat(grad_out), w_out)
    if not share:
        gw = lax.psum(gw, ("rep", "tx", "ty")) * (1.0 / math.sqrt(cells))
    back = lambda a: a.reshape(queries.shape)
    return back(gq), back(gk), back(gv), gw


def solution(mesh):
    tile = P("rep", "tx", "ty", None, None)
    sizes = (mesh.shape["rep"], mesh.shape["tx"], mesh.shape["ty"])
    return jax.shard_map(
        functools.partial(local, sizes),
        mesh=mesh,
        in_specs=(tile, tile, tile, tile, P(), P("tx", "ty")),
        out_specs=(tile, tile, tile, P()),
        check_vma=False,
    )
```

time: 203 us -> 56 us (0.28)
  waiting for transfers between devices: 129 us -> 0 us
  Pallas kernels: 0 us -> 48.1 us
  starting transfers between devices: 19.5 us -> 0 us
  matrix products: 17.8 us -> 0 us
  between operations: 15.4 us -> 1.42 us
  other arithmetic: 6.95 us -> 0 us
  local copies, waits for them, and re-layouts: 11.9 us -> 6.23 us
    psum x1 -> x0, waiting for transfers between devices: 124 us -> none  [local(): grad_w = lax.psum(term, ('rep', 'tx', 'ty')) * (1.0 / math.sqrt(cell_total))]
    pallas_call x0 -> x1, Pallas kernels: none -> 48.1 us  [local(): pl.pallas_call(functools.partial(kernel, (nx, ny, share, cells)), out_sha...]
    ppermute x14 -> x0, starting transfers between devices: 19.5 us -> none  [from_behind(): return lax.ppermute(block, axis, route)]
    dot_general x17 -> x0, matrix products: 13.2 us -> none  [the longest x3 4.18 us: window_grads(): jnp.einsum('qhd,khd->hqk', grad_heads, value_heads, preferred_element_typ...]
    slice x14 -> x0, local copies, waits for them, and re-layouts: 6.75 us -> none  [the longest x4 3.35 us: local(): own[:, half:]]
    ppermute x14 -> x0, waiting for transfers between devices: 5.1 us -> none  [from_behind(): return lax.ppermute(block, axis, route)]
    reshape x4 -> x7, local copies, waits for them, and re-layouts: 0.25 us -> 5.21 us  [the longest x4 3.03 us: local(): flat = lambda a: a.reshape(side, row, a.shape[-1])]
    sub x3 -> x0, matrix products: 4.54 us -> none  [window_grads(): exponent = jnp.exp(scores - row_peak)]
  transfers between devices with their start and end apart: 15 -> 0, of which waited for: 6 -> 0; matrix products, arithmetic and copies ran while one was open for 10% -> 0% of each run, Pallas kernels for 0% -> 0%
where the time goes in v1:
time: 56 us; the launch traced here: 55.8 us
  Pallas kernels  48.1 us (86%)
  local copies, waits for them, and re-layouts  6.23 us (11%)
  between operations  1.42 us (3%)
    pallas_call x1, Pallas kernels, local(): pl.pallas_call(functools.partial(kernel, (nx, ny, share, cells)), out_sha...  48.1 us
    reshape x4, local copies, waits for them, and re-layouts, local(): flat = lambda a: a.reshape(side, row, a.shape[-1])  3.03 us
    reshape x3, local copies, waits for them, and re-layouts, local(): back = lambda a: a.reshape(queries.shape)  2.18 us

profile of v1, /device:TPU:1, one launch (start us, length us, event | category | flops | bytes accessed | tf_op | source)
XLA Modules:
  0.0 55.8 jit_solution(13795284194518178971)
XLA Ops:
  0.6 0.0 copy-start
  0.6 0.0 copy-start.1
  1.4 1.0 %reshape.29.q_in = bf16[8,32,384]{2,1,0:T(8,128)(2,1)S(1)} reshape(bf16[1,8,8,4,384]{4,3,2,1,0:T(4,128)(2,1)} %param.6) | data formatting | bytes 393216 | tf_op jit(solution)/shard_map/reshape | solution.py:278
  2.4 1.0 %reshape.30.k_in = bf16[8,32,384]{2,1,0:T(8,128)(2,1)S(1)} reshape(bf16[1,8,8,4,384]{4,3,2,1,0:T(4,128)(2,1)} %param.7) | data formatting | bytes 393216 | tf_op jit(solution)/shard_map/reshape | solution.py:278
  3.3 1.0 %reshape.31.v_in = bf16[8,32,384]{2,1,0:T(8,128)(2,1)S(1)} reshape(bf16[1,8,8,4,384]{4,3,2,1,0:T(4,128)(2,1)} %param.8) | data formatting | bytes 393216 | tf_op jit(solution)/shard_map/reshape | solution.py:278
  4.3 0.0 copy-done.1
  4.3 0.1 reshape.32.g_in
  4.4 0.0 copy-done
  4.4 48.1 %shard_map.93 = (bf16[8,32,384]{2,1,0:T(8,128)(2,1)S(1)}, bf16[8,32,384]{2,1,0:T(8,128)(2,1)S(1)}, bf16[8,32,384]{2,1,0:T(8,128)(2,1)S(1)}, f32[384,768]{1,0:T(8,128)S(1)}) custom-call(s32[1,1]{1,0:T(1,128)S(6)} %copy.11.fluid, bf16[8,32,384]{2,1,0:T(8,128)(2,1)S(1)} %reshape.29.q_in, bf16[8,32,384]{2,1,0:T(8,128)(2,1)S(1)} %reshape.30.k_in, ...), custom_call_target="tpu_custom_call" | custom-call | tf_op jit(solution)/shard_map/pallas_call | solution.py:282
  52.6 0.7 %reshape.33 = bf16[1,8,8,4,384]{4,3,2,1,0:T(4,128)(2,1)} reshape(bf16[8,32,384]{2,1,0:T(8,128)(2,1)S(1)} %get-tuple-element.8) | data formatting | bytes 393216 | tf_op jit(solution)/shard_map/reshape | solution.py:294
  53.3 0.7 %reshape.34 = bf16[1,8,8,4,384]{4,3,2,1,0:T(4,128)(2,1)} reshape(bf16[8,32,384]{2,1,0:T(8,128)(2,1)S(1)} %get-tuple-element.9) | data formatting | bytes 393216 | tf_op jit(solution)/shard_map/reshape | solution.py:294
  54.0 0.7 %reshape.35 = bf16[1,8,8,4,384]{4,3,2,1,0:T(4,128)(2,1)} reshape(bf16[8,32,384]{2,1,0:T(8,128)(2,1)S(1)} %get-tuple-element.10) | data formatting | bytes 393216 | tf_op jit(solution)/shard_map/reshape | solution.py:294
  54.7 1.0 %copy.12 = f32[384,768]{1,0:T(8,128)} copy(f32[384,768]{1,0:T(8,128)S(1)} %get-tuple-element.19) | data formatting | bytes 2359296
Async XLA Ops:
  0.6 3.8 %copy-start = (bf16[384,768]{1,0:T(8,128)(2,1)S(1)}, bf16[384,768]{1,0:T(8,128)(2,1)}, u32[]{:S(2)}) copy-start(bf16[384,768]{1,0:T(8,128)(2,1)} %w_ref.1) | copy-start | bytes 1769476
  0.6 3.7 %copy-start.1 = (bf16[1,8,8,4,768]{4,3,2,1,0:T(4,128)(2,1)S(1)}, bf16[1,8,8,4,768]{4,3,2,1,0:T(4,128)(2,1)}, u32[]{:S(2)}) copy-start(bf16[1,8,8,4,768]{4,3,2,1,0:T(4,128)(2,1)} %param.9) | copy-start | bytes 1179652

commit v2 on v1

--- a/solution.py
+++ b/solution.py
@@ -126,13 +126,14 @@
 
     returning = []
 
-    def give_back():
+    def give_back(g):
+        at_g = slice(g * LANES, (g + 1) * LANES)
         for f, (src, dst) in enumerate(((gq, oq), (gk, ok), (gv, ov))):
             for n, (home, here) in enumerate(leaving):
                 returning.append(
                     pltpu.make_async_remote_copy(
-                        src_ref=src.at[here], dst_ref=dst.at[home],
-                        send_sem=out_send.at[f, n], recv_sem=out_recv.at[f, n],
+                        src_ref=src.at[(*here, at_g)], dst_ref=dst.at[(*home, at_g)],
+                        send_sem=out_send.at[g, f, n], recv_sem=out_recv.at[g, f, n],
                         device_id=ahead[n], device_id_type=MESH,
                     )
                 )
@@ -145,8 +146,8 @@
     arrive(2)
     arrive(3)
     if share:
-        (tb, sb, r0, s1, s1b, r1, s2, r2, a2, a1, a0) = scratch[14:25]
-        (rep_s, rep_r, tx_s, tx_r, ty_s, ty_r, gy_s, gy_r, gx_s, gx_r, gr_s, gr_r) = scratch[25:]
+        (tb, sb, r0, s1, s1b, r1, s2, s2b, r2, ag) = scratch[14:24]
+        (rep_s, rep_r, tx_s, tx_r, ty_s, ty_r, gy_s, gy_r, gx_s, gx_r, gr_s, gr_r) = scratch[24:]
     rep_copies = []
     half = w_ref.shape[1] // 2
     for g in range(groups):
@@ -189,6 +190,7 @@
     y_peers = [(d, at(0, d)) for d in range(1, ny)]
 
     back(0)
+    give_back(0)
     if share:
         for copy in rep_copies:
             copy.wait_recv()
@@ -199,40 +201,66 @@
             lambda d: s1b.at[lax.rem(tx + d, nx)], lambda d: r1.at[d - 1], x_peers, tx_s, tx_r
         )
     back(1)
+    give_back(1)
     if share:
         total = s1[tx]
         for d, copy in enumerate(x_copies):
             copy.wait_recv()
             total = total + r1[d].astype(F32)
         s2[...] = total.reshape(s2.shape)
+        s2b[...] = s2[...].astype(BF16)
         y_copies = spread(
-            lambda d: s2.at[lax.rem(ty + d, ny)], lambda d: r2.at[d - 1], y_peers, ty_s, ty_r
+            lambda d: s2b.at[lax.rem(ty + d, ny)], lambda d: r2.at[d - 1], y_peers, ty_s, ty_r
         )
     back(2)
+    give_back(2)
     for g in range(3, groups):
         back(g)
-    give_back()
+        give_back(g)
     if share:
         total = s2[ty]
         for d, copy in enumerate(y_copies):
             copy.wait_recv()
-            total = total + r2[d]
-        a2[ty] = total * (1.0 / math.sqrt(cells))
-        for copy in spread(lambda d: a2.at[ty], lambda d: a2.at[ty], y_peers, gy_s, gy_r):
-            copy.wait_recv()
-        a1[tx] = a2[...].reshape(a1.shape[1:]).astype(BF16)
-        for copy in spread(lambda d: a1.at[tx], lambda d: a1.at[tx], x_peers, gx_s, gx_r):
-            copy.wait_recv()
-        a0[rep] = a1[...].reshape(a0.shape[1:])
-        last = pltpu.make_async_remote_copy(
-            src_ref=a0.at[rep], dst_ref=a0.at[rep], send_sem=gr_s, recv_sem=gr_r,
-            device_id={"rep": 1 - rep}, device_id_type=MESH,
-        )
-        last.start()
-        last.wait_recv()
+            total = total + r2[d].astype(F32)
+        ag[rep, tx, ty] = (total * (1.0 / math.sqrt(cells))).astype(BF16)
+
+        def hand(slot, peer, send, recv):
+            copy = pltpu.make_async_remote_copy(
+                src_ref=ag.at[slot], dst_ref=ag.at[slot], send_sem=send, recv_sem=recv,
+                device_id=peer, device_id_type=MESH,
+            )
+            copy.start()
+            sent.append(copy)
+            return copy
+
+        def pass_on(dy):
+            slot = (rep, tx, lax.rem(ty + dy, ny))
+            for d, peer in x_peers:
+                along_x[d, dy] = hand(slot, peer, gx_s.at[d - 1, dy], gx_r.at[d - 1, dy])
+            to_core.append(hand(slot, {"rep": 1 - rep}, gr_s.at[0, dy], gr_r.at[0, dy]))
+
+        along_x, to_core = {}, []
+        along_y = [
+            hand((rep, tx, ty), peer, gy_s.at[d - 1], gy_r.at[d - 1]) for d, peer in y_peers
+        ]
+        pass_on(0)
+        order = list(range(ny - 1, 0, -1))
+        for d in range(1, ny):
+            along_y[d - 1].wait_recv()
+            pass_on(ny - d)
+        for dy in [0] + order:
+            for d in range(1, nx):
+                along_x[d, dy].wait_recv()
+                slot = (rep, lax.rem(tx + nx - d, nx), lax.rem(ty + dy, ny))
+                to_core.append(hand(slot, {"rep": 1 - rep}, gr_s.at[d, dy], gr_r.at[d, dy]))
+        for copy in to_core:
+            copy.wait_recv()
+        wy = ag.shape[3]
         for c in range(2):
-            ow[:, c * half : (c + 1) * half] = a0[c].astype(F32)
-        sent.append(last)
+            for i in range(nx):
+                for j in range(ny):
+                    top = (i * ny + j) * wy
+                    ow[top : top + wy, c * half : (c + 1) * half] = ag[c, i, j].astype(F32)
     for copy in returning:
         copy.wait_recv()
     for copies in arriving:
@@ -256,7 +284,7 @@
         pltpu.VMEM((groups * PER_GROUP, side * row, side * row), F32),
         pltpu.VMEM((groups, side * row, LANES), BF16),
         win, win, win,
-        dma((4, 3)), dma((4, 3)), dma((4,)), dma((3, 3)), dma((3, 3)),
+        dma((4, 3)), dma((4, 3)), dma((4,)), dma((groups, 3, 3)), dma((groups, 3, 3)),
     ]
     if share:
         wx = width // nx
@@ -266,14 +294,13 @@
             pltpu.VMEM((width, half), BF16),
             pltpu.VMEM((nx, wx, half), F32), pltpu.VMEM((nx, wx, half), BF16),
             pltpu.VMEM((nx - 1, wx, half), BF16),
-            pltpu.VMEM((ny, wy, half), F32), pltpu.VMEM((ny - 1, wy, half), F32),
-            pltpu.VMEM((ny, wy, half), F32),
-            pltpu.VMEM((nx, wx, half), BF16),
-            pltpu.VMEM((2, width, half), BF16),
+            pltpu.VMEM((ny, wy, half), F32), pltpu.VMEM((ny, wy, half), BF16),
+            pltpu.VMEM((ny - 1, wy, half), BF16),
+            pltpu.VMEM((2, nx, ny, wy, half), BF16),
             dma((groups,)), dma((groups,)),
             dma((nx - 1,)), dma((nx - 1,)), dma((ny - 1,)), dma((ny - 1,)),
-            dma((ny - 1,)), dma((ny - 1,)), dma((nx - 1,)), dma((nx - 1,)),
-            dma, dma,
+            dma((ny - 1,)), dma((ny - 1,)), dma((nx - 1, ny)), dma((nx - 1, ny)),
+            dma((nx, ny)), dma((nx, ny)),
         ]
     flat = lambda a: a.reshape(side, row, a.shape[-1])
     vmem = pl.BlockSpec(memory_space=pltpu.VMEM)

time: 56 us -> 51.4 us (0.918)
  Pallas kernels: 48.1 us -> 43.6 us
    pallas_call x1, Pallas kernels: 48.1 us -> 43.6 us  [local(): pl.pallas_call(functools.partial(kernel, (nx, ny, share, cells)), out_sha...]
where the time goes in v2:
time: 51.4 us; the launch traced here: 51.2 us
  Pallas kernels  43.6 us (85%)
  local copies, waits for them, and re-layouts  6.23 us (12%)
  between operations  1.42 us (3%)
    pallas_call x1, Pallas kernels, local(): pl.pallas_call(functools.partial(kernel, (nx, ny, share, cells)), out_sha...  43.6 us
    reshape x4, local copies, waits for them, and re-layouts, local(): flat = lambda a: a.reshape(side, row, a.shape[-1])  3.03 us
    reshape x3, local copies, waits for them, and re-layouts, local(): back = lambda a: a.reshape(queries.shape)  2.18 us

profile of v2, /device:TPU:1, one launch (start us, length us, event | category | flops | bytes accessed | tf_op | source)
XLA Modules:
  0.0 51.2 jit_solution(16279539662231971061)
XLA Ops:
  0.6 0.0 copy-start
  0.6 0.0 copy-start.1
  1.4 1.0 %reshape.29.q_in = bf16[8,32,384]{2,1,0:T(8,128)(2,1)S(1)} reshape(bf16[1,8,8,4,384]{4,3,2,1,0:T(4,128)(2,1)} %param.6) | data formatting | bytes 393216 | tf_op jit(solution)/shard_map/reshape | solution.py:305
  2.4 1.0 %reshape.30.k_in = bf16[8,32,384]{2,1,0:T(8,128)(2,1)S(1)} reshape(bf16[1,8,8,4,384]{4,3,2,1,0:T(4,128)(2,1)} %param.7) | data formatting | bytes 393216 | tf_op jit(solution)/shard_map/reshape | solution.py:305
  3.3 1.0 %reshape.31.v_in = bf16[8,32,384]{2,1,0:T(8,128)(2,1)S(1)} reshape(bf16[1,8,8,4,384]{4,3,2,1,0:T(4,128)(2,1)} %param.8) | data formatting | bytes 393216 | tf_op jit(solution)/shard_map/reshape | solution.py:305
  4.3 0.0 copy-done.1
  4.3 0.1 reshape.32.g_in
  4.4 0.0 copy-done
  4.4 43.6 %shard_map.93 = (bf16[8,32,384]{2,1,0:T(8,128)(2,1)S(1)}, bf16[8,32,384]{2,1,0:T(8,128)(2,1)S(1)}, bf16[8,32,384]{2,1,0:T(8,128)(2,1)S(1)}, f32[384,768]{1,0:T(8,128)S(1)}) custom-call(s32[1,1]{1,0:T(1,128)S(6)} %copy.11.fluid, bf16[8,32,384]{2,1,0:T(8,128)(2,1)S(1)} %reshape.29.q_in, bf16[8,32,384]{2,1,0:T(8,128)(2,1)S(1)} %reshape.30.k_in, ...), custom_call_target="tpu_custom_call" | custom-call | tf_op jit(solution)/shard_map/pallas_call | solution.py:309
  48.0 0.7 %reshape.33 = bf16[1,8,8,4,384]{4,3,2,1,0:T(4,128)(2,1)} reshape(bf16[8,32,384]{2,1,0:T(8,128)(2,1)S(1)} %get-tuple-element.8) | data formatting | bytes 393216 | tf_op jit(solution)/shard_map/reshape | solution.py:321
  48.8 0.7 %reshape.34 = bf16[1,8,8,4,384]{4,3,2,1,0:T(4,128)(2,1)} reshape(bf16[8,32,384]{2,1,0:T(8,128)(2,1)S(1)} %get-tuple-element.9) | data formatting | bytes 393216 | tf_op jit(solution)/shard_map/reshape | solution.py:321
  49.5 0.7 %reshape.35 = bf16[1,8,8,4,384]{4,3,2,1,0:T(4,128)(2,1)} reshape(bf16[8,32,384]{2,1,0:T(8,128)(2,1)S(1)} %get-tuple-element.10) | data formatting | bytes 393216 | tf_op jit(solution)/shard_map/reshape | solution.py:321
  50.2 1.0 %copy.12 = f32[384,768]{1,0:T(8,128)} copy(f32[384,768]{1,0:T(8,128)S(1)} %get-tuple-element.19) | data formatting | bytes 2359296
Async XLA Ops:
  0.6 3.8 %copy-start = (bf16[384,768]{1,0:T(8,128)(2,1)S(1)}, bf16[384,768]{1,0:T(8,128)(2,1)}, u32[]{:S(2)}) copy-start(bf16[384,768]{1,0:T(8,128)(2,1)} %w_ref.1) | copy-start | bytes 1769476
  0.6 3.7 %copy-start.1 = (bf16[1,8,8,4,768]{4,3,2,1,0:T(4,128)(2,1)S(1)}, bf16[1,8,8,4,768]{4,3,2,1,0:T(4,128)(2,1)}, u32[]{:S(2)}) copy-start(bf16[1,8,8,4,768]{4,3,2,1,0:T(4,128)(2,1)} %param.9) | copy-start | bytes 1179652

commit v3 on v2

--- a/solution.py
+++ b/solution.py
@@ -21,7 +21,7 @@
     return lax.dot_general(a, b, (dims, ((), ())), preferred_element_type=F32)
 
 
-def kernel(plan, fluid, q_in, k_in, v_in, g_in, w_ref, oq, ok, ov, ow, *scratch):
+def kernel(plan, fluid, qkv, w_ref, oq, ok, ov, ow, *scratch):
     nx, ny, share, cells = plan
     (qw, kw, vw, gw, probs, dw, gq, gk, gv, in_send, in_recv, own_sem, out_send, out_recv) = scratch[:14]
     rep, tx, ty = lax.axis_index("rep"), lax.axis_index("tx"), lax.axis_index("ty")
@@ -48,7 +48,10 @@
     high = (slice(hs, side), slice(hr, row))
     leaving = [(low_x, low_y), (low_y, low_x), (lo, high)]
 
-    fields = [(q_in, qw), (k_in, kw), (v_in, vw), (g_in, gw)]
+    def third(n):
+        return qkv.at[:, :, n * width : (n + 1) * width]
+
+    fields = [(third(0), qw), (third(1), kw), (third(2), vw), (qkv.at[:, :, 3 * width :], gw)]
     owns = []
     for f, (src, dst) in enumerate(fields):
         owns.append(pltpu.make_async_copy(src.at[high], dst.at[lo], own_sem.at[f]))
@@ -309,13 +312,13 @@
     gq, gk, gv, gw = pl.pallas_call(
         functools.partial(kernel, (nx, ny, share, cells)),
         out_shape=(grad, grad, grad, jax.ShapeDtypeStruct((width, model), F32)),
-        in_specs=[pl.BlockSpec(memory_space=pltpu.SMEM), hbm, hbm, hbm, hbm, vmem],
+        in_specs=[pl.BlockSpec(memory_space=pltpu.SMEM), hbm, vmem],
         out_specs=(vmem, vmem, vmem, vmem),
         scratch_shapes=scratch,
         compiler_params=pltpu.CompilerParams(
             collective_id=0, has_side_effects=True, vmem_limit_bytes=40 * 2**20
         ),
-    )(fluid_count, flat(queries), flat(keys), flat(values), flat(grad_out), w_out)
+    )(fluid_count, flat(jnp.concatenate([queries, keys, values, grad_out], axis=4)), w_out)
     if not share:
         gw = lax.psum(gw, ("rep", "tx", "ty")) * (1.0 / math.sqrt(cells))
     back = lambda a: a.reshape(queries.shape)

time: 51.4 us -> 51 us (level)
  local copies, waits for them, and re-layouts: 6.23 us -> 4.25 us
  other arithmetic: 0 us -> 1.64 us
    reshape x4 -> x1, local copies, waits for them, and re-layouts: 3.03 us -> 0.22 us  [local(): flat = lambda a: a.reshape(side, row, a.shape[-1])]
    concatenate x0 -> x1, other arithmetic: none -> 1.64 us  [local(): jnp.concatenate([queries, keys, values, grad_out], axis=4)]
    unnamed x5 -> x3, local copies, waits for them, and re-layouts: 1.02 us -> 1.84 us
where the time goes in v3:
time: 51 us; the launch traced here: 50.8 us
  Pallas kernels  43.6 us (85%)
  local copies, waits for them, and re-layouts  4.25 us (8%)
  other arithmetic  1.64 us (3%)
  between operations  1.3 us (3%)
    pallas_call x1, Pallas kernels, local(): pl.pallas_call(functools.partial(kernel, (nx, ny, share, cells)), out_sha...  43.6 us
    reshape x3, local copies, waits for them, and re-layouts, local(): back = lambda a: a.reshape(queries.shape)  2.18 us
    unnamed x3, local copies, waits for them, and re-layouts  1.84 us
    concatenate x1, other arithmetic, local(): jnp.concatenate([queries, keys, values, grad_out], axis=4)  1.64 us

profile of v3, /device:TPU:1, one launch (start us, length us, event | category | flops | bytes accessed | tf_op | source)
XLA Modules:
  0.0 50.8 jit_solution(15469712318855909978)
XLA Ops:
  1.3 1.6 %pad_maximum_fusion = bf16[1,8,8,4,1920]{4,3,2,1,0:T(4,128)(2,1)S(1)} fusion(bf16[1,8,8,4,768]{4,3,2,1,0:T(4,128)(2,1)} %param.9, bf16[1,8,8,4,384]{4,3,2,1,0:T(4,128)(2,1)} %param.8, bf16[1,8,8,4,384]{4,3,2,1,0:T(4,128)(2,1)} %param.7, bf16[1,8,8,4,384]{4,3,2,1,0:T(4,128)(2,1)} %param.6), kind=kLoop, calls=%fused_computation | loop fusion | flops 3932160 | bytes 1966080 | tf_op jit(solution)/shard_map/concatenate | solution.py:321
  2.9 0.0 copy-start
  2.9 0.2 reshape.20.qkv
  3.2 0.8 %copy-done = bf16[384,768]{1,0:T(8,128)(2,1)S(1)} copy-done((bf16[384,768]{1,0:T(8,128)(2,1)S(1)}, bf16[384,768]{1,0:T(8,128)(2,1)}, u32[]{:S(2)}) %copy-start) | copy-done | bytes 589848
  4.0 43.6 %shard_map.93 = (bf16[8,32,384]{2,1,0:T(8,128)(2,1)S(1)}, bf16[8,32,384]{2,1,0:T(8,128)(2,1)S(1)}, bf16[8,32,384]{2,1,0:T(8,128)(2,1)S(1)}, f32[384,768]{1,0:T(8,128)S(1)}) custom-call(s32[1,1]{1,0:T(1,128)S(6)} %copy.11.fluid, bf16[8,32,1920]{2,1,0:T(8,128)(2,1)S(1)} %reshape.20.qkv, bf16[384,768]{1,0:T(8,128)(2,1)S(1)} %copy-done), custom_call_target="tpu_custom_call" | custom-call | tf_op jit(solution)/shard_map/pallas_call | solution.py:312
  47.6 0.7 %reshape.21 = bf16[1,8,8,4,384]{4,3,2,1,0:T(4,128)(2,1)} reshape(bf16[8,32,384]{2,1,0:T(8,128)(2,1)S(1)} %get-tuple-element.8) | data formatting | bytes 393216 | tf_op jit(solution)/shard_map/reshape | solution.py:324
  48.3 0.7 %reshape.22 = bf16[1,8,8,4,384]{4,3,2,1,0:T(4,128)(2,1)} reshape(bf16[8,32,384]{2,1,0:T(8,128)(2,1)S(1)} %get-tuple-element.9) | data formatting | bytes 393216 | tf_op jit(solution)/shard_map/reshape | solution.py:324
  49.0 0.7 %reshape.23 = bf16[1,8,8,4,384]{4,3,2,1,0:T(4,128)(2,1)} reshape(bf16[8,32,384]{2,1,0:T(8,128)(2,1)S(1)} %get-tuple-element.10) | data formatting | bytes 393216 | tf_op jit(solution)/shard_map/reshape | solution.py:324
  49.8 1.0 %copy.12 = f32[384,768]{1,0:T(8,128)} copy(f32[384,768]{1,0:T(8,128)S(1)} %get-tuple-element.19) | data formatting | bytes 2359296
Async XLA Ops:
  2.9 1.1 %copy-start = (bf16[384,768]{1,0:T(8,128)(2,1)S(1)}, bf16[384,768]{1,0:T(8,128)(2,1)}, u32[]{:S(2)}) copy-start(bf16[384,768]{1,0:T(8,128)(2,1)} %w_ref.1) | copy-start | bytes 1769476

commit v4 on v3

--- a/solution.py
+++ b/solution.py
@@ -193,7 +193,6 @@
     y_peers = [(d, at(0, d)) for d in range(1, ny)]
 
     back(0)
-    give_back(0)
     if share:
         for copy in rep_copies:
             copy.wait_recv()
@@ -203,8 +202,8 @@
         x_copies = spread(
             lambda d: s1b.at[lax.rem(tx + d, nx)], lambda d: r1.at[d - 1], x_peers, tx_s, tx_r
         )
+    give_back(0)
     back(1)
-    give_back(1)
     if share:
         total = s1[tx]
         for d, copy in enumerate(x_copies):
@@ -215,8 +214,10 @@
         y_copies = spread(
             lambda d: s2b.at[lax.rem(ty + d, ny)], lambda d: r2.at[d - 1], y_peers, ty_s, ty_r
         )
+    give_back(1)
     back(2)
-    give_back(2)
+    if not share:
+        give_back(2)
     for g in range(3, groups):
         back(g)
         give_back(g)
@@ -247,6 +248,7 @@
             hand((rep, tx, ty), peer, gy_s.at[d - 1], gy_r.at[d - 1]) for d, peer in y_peers
         ]
         pass_on(0)
+        give_back(2)
         order = list(range(ny - 1, 0, -1))
         for d in range(1, ny):
             along_y[d - 1].wait_recv()

time: 51 us -> 50.5 us (level)
  no operation moved by 1% of the time
where the time goes in v4:
time: 50.5 us; the launch traced here: 50.3 us
  Pallas kernels  43.1 us (85%)
  local copies, waits for them, and re-layouts  4.25 us (8%)
  other arithmetic  1.64 us (3%)
  between operations  1.3 us (3%)
    pallas_call x1, Pallas kernels, local(): pl.pallas_call(functools.partial(kernel, (nx, ny, share, cells)), out_sha...  43.1 us
    reshape x3, local copies, waits for them, and re-layouts, local(): back = lambda a: a.reshape(queries.shape)  2.18 us
    unnamed x3, local copies, waits for them, and re-layouts  1.84 us
    concatenate x1, other arithmetic, local(): jnp.concatenate([queries, keys, values, grad_out], axis=4)  1.64 us

profile of v4, /device:TPU:1, one launch (start us, length us, event | category | flops | bytes accessed | tf_op | source)
XLA Modules:
  0.0 50.3 jit_solution(5058325103948392726)
XLA Ops:
  1.3 1.6 %pad_maximum_fusion = bf16[1,8,8,4,1920]{4,3,2,1,0:T(4,128)(2,1)S(1)} fusion(bf16[1,8,8,4,768]{4,3,2,1,0:T(4,128)(2,1)} %param.9, bf16[1,8,8,4,384]{4,3,2,1,0:T(4,128)(2,1)} %param.8, bf16[1,8,8,4,384]{4,3,2,1,0:T(4,128)(2,1)} %param.7, bf16[1,8,8,4,384]{4,3,2,1,0:T(4,128)(2,1)} %param.6), kind=kLoop, calls=%fused_computation | loop fusion | flops 3932160 | bytes 1966080 | tf_op jit(solution)/shard_map/concatenate | solution.py:323
  2.9 0.0 copy-start
  2.9 0.2 reshape.20.qkv
  3.2 0.8 %copy-done = bf16[384,768]{1,0:T(8,128)(2,1)S(1)} copy-done((bf16[384,768]{1,0:T(8,128)(2,1)S(1)}, bf16[384,768]{1,0:T(8,128)(2,1)}, u32[]{:S(2)}) %copy-start) | copy-done | bytes 589848
  4.0 43.1 %shard_map.93 = (bf16[8,32,384]{2,1,0:T(8,128)(2,1)S(1)}, bf16[8,32,384]{2,1,0:T(8,128)(2,1)S(1)}, bf16[8,32,384]{2,1,0:T(8,128)(2,1)S(1)}, f32[384,768]{1,0:T(8,128)S(1)}) custom-call(s32[1,1]{1,0:T(1,128)S(6)} %copy.11.fluid, bf16[8,32,1920]{2,1,0:T(8,128)(2,1)S(1)} %reshape.20.qkv, bf16[384,768]{1,0:T(8,128)(2,1)S(1)} %copy-done), custom_call_target="tpu_custom_call" | custom-call | tf_op jit(solution)/shard_map/pallas_call | solution.py:314
  47.1 0.7 %reshape.21 = bf16[1,8,8,4,384]{4,3,2,1,0:T(4,128)(2,1)} reshape(bf16[8,32,384]{2,1,0:T(8,128)(2,1)S(1)} %get-tuple-element.8) | data formatting | bytes 393216 | tf_op jit(solution)/shard_map/reshape | solution.py:326
  47.8 0.7 %reshape.22 = bf16[1,8,8,4,384]{4,3,2,1,0:T(4,128)(2,1)} reshape(bf16[8,32,384]{2,1,0:T(8,128)(2,1)S(1)} %get-tuple-element.9) | data formatting | bytes 393216 | tf_op jit(solution)/shard_map/reshape | solution.py:326
  48.6 0.7 %reshape.23 = bf16[1,8,8,4,384]{4,3,2,1,0:T(4,128)(2,1)} reshape(bf16[8,32,384]{2,1,0:T(8,128)(2,1)S(1)} %get-tuple-element.10) | data formatting | bytes 393216 | tf_op jit(solution)/shard_map/reshape | solution.py:326
  49.3 1.0 %copy.12 = f32[384,768]{1,0:T(8,128)} copy(f32[384,768]{1,0:T(8,128)S(1)} %get-tuple-element.19) | data formatting | bytes 2359296
Async XLA Ops:
  2.9 1.1 %copy-start = (bf16[384,768]{1,0:T(8,128)(2,1)S(1)}, bf16[384,768]{1,0:T(8,128)(2,1)}, u32[]{:S(2)}) copy-start(bf16[384,768]{1,0:T(8,128)(2,1)} %w_ref.1) | copy-start | bytes 1769476
